TPU v7x, 256 devices: a whole 4x4x8 slice. The times are simulated.
256 devices in a mesh: tm: 32 (over y_lo, z, core), net: 8 (over x, y_hi).
Axes of the slice: x: 4, y: 4 (y_hi: 2, y_lo: 2; y = y_hi * 2 + y_lo), z: 8, core: 2. Of those that a mesh axis runs over, the one named last changes fastest.
Arguments:
- demand: float32 [4096, 12288], P('net', 'tm'), may hold values from 0.5 to 1.5
- availability: float32 [4096, 12288], P('net', 'tm'), may hold values from 0.05 to 1
- gen_cost: float32 [4096], P('net'), may hold values from 0.2 to 2
- cap_cost: float32 [4096], P('net'), may hold values from 1228.8 to 7372.8
- runoff: bfloat16 [32768, 12288], P('net', 'tm'), may hold values from 0.0099487305 to 1
- cell_plant: int32 [32768], P('net'), may hold values from 0 to 1799, as said below
- plant_bus: int32 [1800], P('net'), may hold values from 0 to 511
- store_cap: float32 [1800], P('net'), may hold values from 1 to 4
- line_from: int32 [5120], P('net'), may hold values from 0 to 511
- line_to: int32 [5120], P('net'), may hold values from 0 to 511
- line_cap: float32 [5120], P('net'), may hold values from 0.5 to 2
- cut_from: int32 [1024], P('net'), may hold values from 0 to 511
- cut_to: int32 [1024], P('net'), may hold values from 0 to 511
- cut_cap: float32 [1024], P('net'), may hold values from 0.5 to 2
- generation: float32 [4096, 12288], P('net', 'tm'), may hold values from 0 to 2
- capacity: float32 [4096], P('net'), may hold values from 0.05 to 2
- release: float32 [1800, 12288], P('net', 'tm'), may hold values from 0 to 1
- storage_level: float32 [1800, 12288], P('net', 'tm'), may hold values from 0 to 2
- line_flow: float32 [5120, 12288], P('net', 'tm'), may hold values from -6 to 6
- cut_flow: float32 [1024, 12288], P('net', 'tm'), may hold values from -6 to 6
- dual_bal: float32 [4096, 12288], P('net', 'tm'), may hold values from -6 to 6
- dual_cap: float32 [4096, 12288], P('net', 'tm'), may hold values from 0 to 2.25, as said below
- dual_sto: float32 [1800, 12288], P('net', 'tm'), may hold values from -6 to 6
Outputs:
- new_generation: float32 [4096, 12288], P('net', 'tm')
- new_capacity: float32 [4096], P('net')
- new_release: float32 [1800, 12288], P('net', 'tm')
- new_level: float32 [1800, 12288], P('net', 'tm')
- new_flow: float32 [5120, 12288], P('net', 'tm')
- new_cut_flow: float32 [1024, 12288], P('net', 'tm')
- new_dual_bal: float32 [4096, 12288], P('net', 'tm')
- new_dual_cap: float32 [4096, 12288], P('net', 'tm')
- new_dual_sto: float32 [1800, 12288], P('net', 'tm')
Inputs may be any that keep to these rules, and one draw needn't show every extreme that they name: `cell_plant`: plant numbers; cell c lies in zone floor(c / 4096) and drains into a plant of that zone, of the zone before it or of the zone after it (zones taken cyclically, plant p in zone floor(p / 225)). `plant_bus`: bus numbers within the plant's zone. `line_from`: bus numbers within the line's zone. `line_to`: bus numbers within the line's zone. `cut_from`: bus numbers within the cut line's own zone. `dual_cap`: nonnegative.
All inputs are finite; a program needn't handle non-finite values.
Results may differ from a plain program's by a relative error of at most 0.0003.
Values sent between devices are 32-bit elements; how exact they have to be, the bound alone decides.
A program may use at most 64 MiB of HBM per device.

v0:
```python
import jax
import jax.numpy as jnp
from jax import lax
from jax.experimental import pallas as pl
from jax.experimental.pallas import tpu as pltpu
from jax.sharding import PartitionSpec as P

MESH = pl.DeviceIdType.MESH
PRIMAL = 0.4
DUAL = 0.4
W = 128
F32 = jnp.float32
BF16 = jnp.bfloat16


def split(values):
    hi = values.astype(BF16)
    lo = (values - hi.astype(F32)).astype(BF16)
    return jnp.concatenate([hi, lo], axis=1)


def joined(product):
    return product[:, :W] + product[:, W:]


def dot(a, b):
    return jnp.dot(a, b, preferred_element_type=F32)


def columns(row):
    blocks = []
    for i in range(row.shape[1] // W):
        blocks.append(jnp.transpose(jnp.broadcast_to(row[:, i * W : (i + 1) * W], (W, W))))
    return jnp.concatenate(blocks, axis=0) if len(blocks) > 1 else blocks[0]


def wide(block, count):
    return jnp.concatenate([block] * count, axis=1) if count > 1 else block


def make_kernel(sizes):
    buses, plants, lines, cuts, cells, hours, times, zones = sizes
    chunks = hours // W
    pad = -(-plants // W) * W
    prow = -(-plants // 16) * 16
    srow = -(-plants // 8) * 8
    parts = 4
    depth = cells // parts
    L0, F0, T0, P0 = 0, lines, lines + cuts, lines + 2 * cuts
    rows = P0 + pad
    i_to, i_from, i_cf, i_ct, i_pl = 0, lines, 2 * lines, 2 * lines + cuts, 2 * lines + 2 * cuts
    c_gen, c_line, c_cut, c_sto = 0, buses, buses + lines, buses + lines + cuts
    r_cost, r_cap = c_sto + pad, c_sto + pad + buses
    cap_step = PRIMAL / (hours * times)

    def kernel(
        ints, floats, cell,
        h_dem, h_av, h_run, h_gen, h_rel, h_lev, h_lf, h_cf, h_bal, h_dc, h_ds,
        o_gen, o_cap, o_rel, o_lev, o_lf, o_cf, o_bal, o_dc, o_ds,
        dem, av, run, gen, rel, lev, lf, cf, bal, dc, ds,
        inc, inct, bars, gbar, lbar, colf, padr, dcut, far, near, own,
        x_ct, x_ds, x_lb, s_p, x_p, s_b, x_b, x_far, x_inf, slots,
        isem, ct_s, ct_r, ds_s, ds_r, lb_s, lb_r, p_s, p_r, b_s, b_r, far_s, far_r, inf_s, inf_r, ps_s, ps_r,
    ):
        t = lax.axis_index("tm")
        q = lax.axis_index("net")
        qn = lax.rem(q + 1, zones)
        qp = lax.rem(q + zones - 1, zones)
        sign = 1 - 2 * lax.rem(q, 2)
        mate = q + sign
        far_zone = lax.rem(q - sign + zones, zones)
        far_to = lax.rem(q - 2 * sign + zones, zones)
        tn = lax.rem(t + 1, times)
        tp = lax.rem(t + times - 1, times)

        loads = {}
        pairs = [
            ("ds", h_ds, ds), ("bal", h_bal, bal), ("av", h_av, av), ("dc", h_dc, dc),
        ]
        for k in range(parts):
            at = pl.ds(k * depth, depth)
            pairs.append((("run", k), h_run.at[at], run.at[at]))
        pairs += [
            ("cf", h_cf, cf), ("lf", h_lf, lf), ("rel", h_rel, rel), ("gen", h_gen, gen),
            ("lev", h_lev, lev), ("dem", h_dem, dem),
        ]
        for n, (name, src, dst) in enumerate(pairs):
            loads[name] = pltpu.make_async_copy(src, dst, isem.at[n])
            loads[name].start()

        barrier = pltpu.get_barrier_semaphore()

        def greet(i, carry):
            pl.semaphore_signal(
                barrier, inc=1, device_id=(lax.rem(t + i, times), q), device_id_type=MESH
            )
            return carry

        lax.fori_loop(1, times, greet, 0)
        for d in (1, 2, zones - 2, zones - 1):
            pl.semaphore_signal(
                barrier, inc=1, device_id=(t, lax.rem(q + d, zones)), device_id_type=MESH
            )
        pl.semaphore_wait(barrier, times + 3)

        sent = []

        def send(src, dst, ssem, rsem, tt, qq):
            copy = pltpu.make_async_remote_copy(
                src_ref=src, dst_ref=dst, send_sem=ssem, recv_sem=rsem,
                device_id=(tt, qq), device_id_type=MESH,
            )
            copy.start()
            sent.append(copy)
            return copy

        def lanes(c):
            return slice(c * W, (c + 1) * W)

        k_ct = send(ints.at[:, pl.ds(i_ct, cuts)], x_ct, ct_s, ct_r, t, qn)
        loads["ds"].wait()
        k_ds = [send(ds.at[:, pl.ds(0, W)], x_ds.at[0], ds_s.at[0], ds_r.at[0], tp, q)]

        def price_out(k, dual_of):
            total = None
            for c in range(chunks):
                term = av[:, lanes(c)] * dual_of(c)
                total = term if total is None else total + term
            row = jnp.concatenate(
                [
                    jnp.sum(jnp.transpose(total[i * W : (i + 1) * W]), axis=0, keepdims=True)
                    for i in range(buses // W)
                ],
                axis=1,
            )
            slots[k, 0] = row

            def out(i, carry):
                pltpu.make_async_remote_copy(
                    src_ref=slots.at[k, 0], dst_ref=slots.at[k, i],
                    send_sem=ps_s.at[k], recv_sem=ps_r.at[k],
                    device_id=(lax.rem(t + i, times), q), device_id_type=MESH,
                ).start()
                return carry

            lax.fori_loop(1, times, out, 0)

        def price_all(k):
            everyone = slots.at[k, pl.ds(1, times - 1)]
            whole = pltpu.make_async_remote_copy(
                src_ref=everyone, dst_ref=everyone, send_sem=ps_s.at[k], recv_sem=ps_r.at[k],
                device_id=(tn, q), device_id_type=MESH,
            )
            whole.wait_recv()
            total = slots[k, lax.rem(t + times, times)]
            for j in range(1, times):
                total = total + slots[k, lax.rem(t - j + times, times)]
            whole.wait_send()
            return total

        loads["av"].wait()
        loads["dc"].wait()
        price_out(0, lambda c: dc[:, lanes(c)])

        lane_bus = lax.broadcasted_iota(jnp.int32, (W, buses), 1)
        row_bus = lax.broadcasted_iota(jnp.int32, (buses, W), 0)
        one, zero = F32(1.0), F32(0.0)

        def flags(mask):
            return jnp.where(mask, one, zero)

        def place(at, to_row, from_row):
            m = jnp.zeros((W, buses), F32)
            mt = jnp.zeros((buses, W), F32)
            if to_row is not None:
                m = m + flags(wide(columns(to_row), buses // W) == lane_bus)
                mt = mt + flags(to_row == row_bus)
            if from_row is not None:
                m = m - flags(wide(columns(from_row), buses // W) == lane_bus)
                mt = mt - flags(from_row == row_bus)
            inc[at : at + W, :] = m.astype(BF16)
            inct[:, at : at + W] = mt.astype(BF16)

        for i in range(lines // W):
            place(
                L0 + i * W,
                ints[:, i_to + i * W : i_to + (i + 1) * W],
                ints[:, i_from + i * W : i_from + (i + 1) * W],
            )
        for i in range(cuts // W):
            place(F0 + i * W, None, ints[:, i_cf + i * W : i_cf + (i + 1) * W])
        for i in range(pad // W):
            place(P0 + i * W, ints[:, i_pl + i * W : i_pl + (i + 1) * W], None)
        for i in range(r_cost // W):
            colf[i * W : (i + 1) * W, :] = columns(floats[:, i * W : (i + 1) * W])
        padr[...] = jnp.zeros_like(padr)

        k_ct.wait_recv()
        for i in range(cuts // W):
            place(T0 + i * W, x_ct[:, i * W : (i + 1) * W], None)

        loads["bal"].wait()
        k_p, k_b = [], []

        def send_prices(k, c, value):
            s_p[k, c] = joined(dot(inc[T0:P0, :], value))
            k_p.append(send(s_p.at[k, c], x_p.at[k, c], p_s.at[k, c], p_r.at[k, c], t, qp))

        for c in range(chunks):
            send_prices(0, c, split(bal[:, lanes(c)]))

        def terms(zone, out):
            ids = lax.broadcasted_iota(jnp.int32, (prow, depth), 0) + zone * plants
            total = None
            for k in range(parts):
                if ("run", k) in loads:
                    loads.pop(("run", k)).wait()
                onehot = flags(ids == cell[:, k * depth : (k + 1) * depth]).astype(BF16)
                term = dot(onehot, run[k * depth : (k + 1) * depth, :])
                total = term if total is None else total + term
            for c in range(chunks):
                out[c] = total[:, lanes(c)]

        terms(far_zone, far)
        k_far = [
            send(far.at[c, pl.ds(0, srow)], x_far.at[c], far_s.at[c], far_r.at[c], t, far_to)
            for c in range(chunks)
        ]

        loads["cf"].wait()
        loads["lf"].wait()
        loads["rel"].wait()

        def bound(v, b):
            return jnp.minimum(jnp.maximum(v, -b), b)

        def line_step(c, value, flow, flow_out):
            diff = joined(dot(inc[L0:T0, :], value))
            cap = colf[c_line : c_line + lines, :]
            old = flow[:, lanes(c)]
            new = bound(old + PRIMAL * diff[:lines], cap)
            bars[c, L0 : L0 + lines, :] = split(2.0 * new - old)
            flow_out[:, lanes(c)] = new
            dcut[:, lanes(c)] = diff[lines:]

        def cut_step(k, c, flow, flow_out):
            k_p[k * chunks + c].wait_recv()
            cap = colf[c_cut : c_cut + cuts, :]
            old = flow[:, lanes(c)]
            new = bound(old + PRIMAL * (x_p[k, c] + dcut[:, lanes(c)]), cap)
            bar = 2.0 * new - old
            flow_out[:, lanes(c)] = new
            s_b[k, c] = bar
            k_b.append(send(s_b.at[k, c], x_b.at[k, c], b_s.at[k, c], b_r.at[k, c], t, qn))
            bars[c, F0 : F0 + cuts, :] = split(bar)

        def cut_in(k, c):
            k_b[k * chunks + c].wait_recv()
            bars[c, T0 : T0 + cuts, :] = split(x_b[k, c])

        def plant_prices(c, value):
            return joined(dot(inc[P0 : P0 + pad, :], value))[:plants]

        def release_step(c, price, old_ref, dual_ref, out_ref):
            old = old_ref[:, lanes(c)]
            new = jnp.maximum(0.0, old + PRIMAL * (price + dual_ref[:, lanes(c)]))
            bar = 2.0 * new - old
            out_ref[:, lanes(c)] = new
            padr[0:plants, :] = bar
            bars[c, P0 : P0 + pad, :] = split(padr[...])
            return bar

        def gen_step(c, old_ref, price_ref, dual_ref, out_ref):
            cost = colf[c_gen : c_gen + buses, :]
            old = old_ref[:, lanes(c)]
            new = jnp.maximum(
                0.0, old - PRIMAL * (cost - price_ref[:, lanes(c)] + dual_ref[:, lanes(c)])
            )
            gbar[:, lanes(c)] = 2.0 * new - old
            out_ref[:, lanes(c)] = new

        lane = lax.broadcasted_iota(jnp.int32, (plants, W), 1)

        def level_step(k, dual_ref, old_ref, out_ref):
            cap = colf[c_sto : c_sto + pad, :][:plants]
            rolled = [pltpu.roll(dual_ref[:, lanes(c)], W - 1, 1) for c in range(chunks)]
            rolled.append(pltpu.roll(x_ds[k], W - 1, 1))
            for c in range(chunks):
                after = jnp.where(lane == W - 1, rolled[c + 1], rolled[c])
                old = old_ref[:, lanes(c)]
                new = jnp.minimum(
                    jnp.maximum(old + PRIMAL * (dual_ref[:, lanes(c)] - after), 0.0), cap
                )
                lbar[k, :, lanes(c)] = 2.0 * new - old
                out_ref[:, lanes(c)] = new
            return send(
                lbar.at[k, :, pl.ds(hours - W, W)], x_lb.at[k], lb_s.at[k], lb_r.at[k], tn, q
            )

        def storage_step(k, dual_ref, relbars, out_ref):
            rolled = [pltpu.roll(x_lb[k], 1, 1)]
            rolled += [pltpu.roll(lbar[k, :, lanes(c)], 1, 1) for c in range(chunks)]
            for c in range(chunks):
                before = jnp.where(lane == 0, rolled[c], rolled[c + 1])
                inflow = own[c][:plants]
                out_ref[:, lanes(c)] = dual_ref[:, lanes(c)] + DUAL * (
                    inflow - lbar[k, :, lanes(c)] + before - relbars(c)
                )

        def balance_step(c, old_ref, out_ref):
            balance = gbar[:, lanes(c)] + joined(dot(inct[...], bars[c]))
            out_ref[:, lanes(c)] = old_ref[:, lanes(c)] + DUAL * (dem[:, lanes(c)] - balance)

        def cap_dual_step(cap_bar, dual_ref, out_ref):
            col = columns(cap_bar)
            for c in range(chunks):
                out_ref[:, lanes(c)] = jnp.maximum(
                    0.0,
                    dual_ref[:, lanes(c)] - DUAL * (av[:, lanes(c)] * col - gbar[:, lanes(c)]),
                )

        for c in range(chunks):
            line_step(c, split(bal[:, lanes(c)]), lf, o_lf)
        for c in range(chunks):
            cut_step(0, c, cf, o_cf)
        for c in range(chunks):
            release_step(c, plant_prices(c, split(bal[:, lanes(c)])), rel, ds, o_rel)

        terms(mate, near)
        k_inf = []
        for c in range(chunks):
            k_far[c].wait_recv()
            near[c, 0:srow, :] = near[c, 0:srow, :] + x_far[c]
            k_inf.append(
                send(near.at[c, pl.ds(0, srow)], x_inf.at[c], inf_s.at[c], inf_r.at[c], t, mate)
            )

        loads["gen"].wait()
        for c in range(chunks):
            gen_step(c, gen, bal, dc, o_gen)
        loads["lev"].wait()
        k_ds[0].wait_recv()
        k_lb = [level_step(0, ds, lev, o_lev)]

        cost = floats[:, r_cost : r_cost + buses]
        cap_old = floats[:, r_cap : r_cap + buses]
        cap_one = jnp.maximum(0.0, cap_old - cap_step * (cost - price_all(0)))
        cap_dual_step(2.0 * cap_one - cap_old, dc, o_dc)
        price_out(1, lambda c: o_dc[:, lanes(c)])

        terms(q, own)

        loads["dem"].wait()
        for c in range(chunks):
            cut_in(0, c)
            balance_step(c, bal, o_bal)
            send_prices(1, c, split(o_bal[:, lanes(c)]))

        for c in range(chunks):
            line_step(c, split(o_bal[:, lanes(c)]), o_lf, o_lf)
        for c in range(chunks):
            cut_step(1, c, o_cf, o_cf)
        for c in range(chunks):
            k_inf[c].wait_recv()
            own[c, 0:srow, :] = own[c, 0:srow, :] + x_inf[c]
        k_lb[0].wait_recv()
        storage_step(0, ds, lambda c: 2.0 * o_rel[:, lanes(c)] - rel[:, lanes(c)], o_ds)
        k_ds.append(send(o_ds.at[:, pl.ds(0, W)], x_ds.at[1], ds_s.at[1], ds_r.at[1], tp, q))
        relbar = [
            release_step(c, plant_prices(c, split(o_bal[:, lanes(c)])), o_rel, o_ds, o_rel)
            for c in range(chunks)
        ]
        for c in range(chunks):
            gen_step(c, o_gen, o_bal, o_dc, o_gen)
        cap_two = jnp.maximum(0.0, cap_one - cap_step * (cost - price_all(1)))
        o_cap[...] = cap_two
        cap_dual_step(2.0 * cap_two - cap_one, o_dc, o_dc)
        k_ds[1].wait_recv()
        k_lb.append(level_step(1, o_ds, o_lev, o_lev))
        k_lb[1].wait_recv()
        k_ds[1].wait_send()
        storage_step(1, o_ds, lambda c: relbar[c], o_ds)
        for c in range(chunks):
            cut_in(1, c)
            balance_step(c, o_bal, o_bal)
        for copy in sent:
            if copy is not k_ds[1]:
                copy.wait_send()

    def big(n, kind=F32):
        return pltpu.VMEM((n, hours), kind)

    dma = pltpu.SemaphoreType.DMA
    scratch = [
        big(buses), big(buses), big(cells, BF16), big(buses), big(plants), big(plants),
        big(lines), big(cuts), big(buses), big(buses), big(plants),
        pltpu.VMEM((rows, buses), BF16),
        pltpu.VMEM((buses, rows), BF16),
        pltpu.VMEM((chunks, rows, 2 * W), BF16),
        big(buses),
        pltpu.VMEM((2, plants, hours), F32),
        pltpu.VMEM((r_cost, W), F32),
        pltpu.VMEM((pad, W), F32),
        big(cuts),
        pltpu.VMEM((chunks, prow, W), F32),
        pltpu.VMEM((chunks, prow, W), F32),
        pltpu.VMEM((chunks, prow, W), F32),
        pltpu.VMEM((1, cuts), jnp.int32),
        pltpu.VMEM((2, plants, W), F32),
        pltpu.VMEM((2, plants, W), F32),
        pltpu.VMEM((2, chunks, cuts, W), F32),
        pltpu.VMEM((2, chunks, cuts, W), F32),
        pltpu.VMEM((2, chunks, cuts, W), F32),
        pltpu.VMEM((2, chunks, cuts, W), F32),
        pltpu.VMEM((chunks, srow, W), F32),
        pltpu.VMEM((chunks, srow, W), F32),
        pltpu.VMEM((2, times, 1, buses), F32),
        dma((10 + parts,)),
        dma, dma, dma((2,)), dma((2,)), dma((2,)), dma((2,)),
        dma((2, chunks)), dma((2, chunks)), dma((2, chunks)), dma((2, chunks)),
        dma((chunks,)), dma((chunks,)), dma((chunks,)), dma((chunks,)),
        dma((2,)), dma((2,)),
    ]
    return kernel, scratch, pad


def solution(mesh):
    times, zones = mesh.shape["tm"], mesh.shape["net"]

    def local(
        demand, availability, gen_cost, cap_cost, runoff, cell_plant, plant_bus, store_cap,
        line_from, line_to, line_cap, cut_from, cut_to, cut_cap, generation, capacity,
        release, storage_level, line_flow, cut_flow, dual_bal, dual_cap, dual_sto,
    ):
        buses, hours = demand.shape
        plants, lines, cuts, cells = (
            release.shape[0], line_flow.shape[0], cut_flow.shape[0], runoff.shape[0],
        )
        kernel, scratch, pad = make_kernel((buses, plants, lines, cuts, cells, hours, times, zones))
        more = pad - plants
        ints = jnp.concatenate(
            [line_to, line_from, cut_from, cut_to, jnp.pad(plant_bus, (0, more), constant_values=-1)]
        ).reshape(1, -1)
        floats = jnp.concatenate(
            [gen_cost, line_cap, cut_cap, jnp.pad(store_cap, (0, more)), cap_cost, capacity]
        ).reshape(1, -1)
        vmem = pl.BlockSpec(memory_space=pltpu.VMEM)
        hbm = pl.BlockSpec(memory_space=pl.ANY)

        def shape(n):
            return jax.ShapeDtypeStruct((n, hours), F32)

        outs = pl.pallas_call(
            kernel,
            out_shape=(
                shape(buses), jax.ShapeDtypeStruct((1, buses), F32), shape(plants), shape(plants),
                shape(lines), shape(cuts), shape(buses), shape(buses), shape(plants),
            ),
            in_specs=[vmem] * 3 + [hbm] * 11,
            out_specs=(vmem,) * 9,
            scratch_shapes=scratch,
            compiler_params=pltpu.CompilerParams(
                collective_id=0, has_side_effects=True, vmem_limit_bytes=48 << 20
            ),
        )(
            ints, floats, cell_plant.reshape(1, -1),
            demand, availability, runoff, generation, release, storage_level, line_flow, cut_flow,
            dual_bal, dual_cap, dual_sto,
        )
        outs = list(outs)
        outs[1] = outs[1].reshape(buses)
        return tuple(outs)

    both, net = P("net", "tm"), P("net")
    in_specs = (both, both, net, net, both) + (net,) * 9 + (both, net) + (both,) * 7
    out_specs = (both, net) + (both,) * 7
    return jax.shard_map(local, mesh=mesh, in_specs=in_specs, out_specs=out_specs, check_vma=False)
```

profile of v0, /device:TPU:2, one launch (start us, length us, event | category | flops | bytes accessed | tf_op | source)
XLA Modules:
  0.0 81.1 jit_solution(5529888315389565602)
XLA Ops:
  0.7 0.7 constant_dynamic-update-slice_fusion.4
  1.3 0.7 constant_dynamic-update-slice_fusion.7
  2.0 0.7 constant_dynamic-update-slice_fusion.2
  3.4 0.7 constant_dynamic-update-slice_fusion
  4.1 0.7 constant_dynamic-update-slice_fusion.5
  4.8 0.7 constant_dynamic-update-slice_fusion.10
  6.1 0.7 constant_dynamic-update-slice_fusion.3
  6.8 0.7 constant_dynamic-update-slice_fusion.1
  7.5 0.7 constant_dynamic-update-slice_fusion.8
  8.2 1.1 %copy-done = f32[512,384]{1,0:T(8,128)S(1)} copy-done((f32[512,384]{1,0:T(8,128)S(1)}, f32[512,384]{1,0:T(8,128)}, u32[]{:S(2)}) %copy-start) | copy-done | bytes 786456
  9.3 1.0 %copy-done.1 = f32[225,384]{1,0:T(8,128)S(1)} copy-done((f32[225,384]{1,0:T(8,128)S(1)}, f32[225,384]{1,0:T(8,128)}, u32[]{:S(2)}) %copy-start.1) | copy-done | bytes 345624
  10.3 1.0 %copy-done.2 = f32[225,384]{1,0:T(8,128)S(1)} copy-done((f32[225,384]{1,0:T(8,128)S(1)}, f32[225,384]{1,0:T(8,128)}, u32[]{:S(2)}) %copy-start.2) | copy-done | bytes 345624
  11.3 1.0 %copy-done.3 = f32[225,384]{1,0:T(8,128)S(1)} copy-done((f32[225,384]{1,0:T(8,128)S(1)}, f32[225,384]{1,0:T(8,128)}, u32[]{:S(2)}) %copy-start.3) | copy-done | bytes 345624
  12.3 0.9 %copy-done.4 = f32[128,384]{1,0:T(8,128)S(1)} copy-done((f32[128,384]{1,0:T(8,128)S(1)}, f32[128,384]{1,0:T(8,128)}, u32[]{:S(2)}) %copy-start.4) | copy-done | bytes 196632
  13.2 0.7 copy-done.5
  13.9 60.1 %shard_map.286 = (f32[512,384]{1,0:T(8,128)S(1)}, f32[1,512]{1,0:T(1,128)S(1)}, f32[225,384]{1,0:T(8,128)S(1)}, f32[225,384]{1,0:T(8,128)S(1)}, f32[640,384]{1,0...) custom-call(s32[1,1792]{1,0:T(1,128)S(1)} %reshape.30.ints, ...), custom_call_target="tpu_custom_call" | custom-call | tf_op jit(solution)/shard_map/pallas_call | solution.py:453
  74.0 0.9 %copy.52 = f32[512,384]{1,0:T(8,128)} copy(f32[512,384]{1,0:T(8,128)S(1)} %get-tuple-element.36) | data formatting | bytes 1572864
  75.5 0.7 copy.54
  76.2 0.7 copy.55
  77.0 0.9 %copy.56 = f32[640,384]{1,0:T(8,128)} copy(f32[640,384]{1,0:T(8,128)S(1)} %copy-done.6) | data formatting | bytes 1966080
  77.9 0.7 copy.57
  78.6 0.9 %copy.58 = f32[512,384]{1,0:T(8,128)} copy(f32[512,384]{1,0:T(8,128)S(1)} %get-tuple-element.42) | data formatting | bytes 1572864
  79.5 0.9 %copy.59 = f32[512,384]{1,0:T(8,128)} copy(f32[512,384]{1,0:T(8,128)S(1)} %get-tuple-element.43) | data formatting | bytes 1572864
  80.3 0.7 copy.60
  (15 shorter events, 1.9 us)
Async XLA Ops:
  8.2 1.1 %copy-start = (f32[512,384]{1,0:T(8,128)S(1)}, f32[512,384]{1,0:T(8,128)}, u32[]{:S(2)}) copy-start(f32[512,384]{1,0:T(8,128)} %h_dem.1) | copy-start | bytes 2359300
  9.3 1.0 %copy-start.1 = (f32[225,384]{1,0:T(8,128)S(1)}, f32[225,384]{1,0:T(8,128)}, u32[]{:S(2)}) copy-start(f32[225,384]{1,0:T(8,128)} %h_rel.1) | copy-start | bytes 1036804
  10.3 1.0 %copy-start.2 = (f32[225,384]{1,0:T(8,128)S(1)}, f32[225,384]{1,0:T(8,128)}, u32[]{:S(2)}) copy-start(f32[225,384]{1,0:T(8,128)} %h_lev.1) | copy-start | bytes 1036804
  11.3 1.0 %copy-start.3 = (f32[225,384]{1,0:T(8,128)S(1)}, f32[225,384]{1,0:T(8,128)}, u32[]{:S(2)}) copy-start(f32[225,384]{1,0:T(8,128)} %h_ds.1) | copy-start | bytes 1036804
  12.3 0.9 %copy-start.4 = (f32[128,384]{1,0:T(8,128)S(1)}, f32[128,384]{1,0:T(8,128)}, u32[]{:S(2)}) copy-start(f32[128,384]{1,0:T(8,128)} %h_cf.1) | copy-start | bytes 589828
  13.2 0.7 copy-start.5
  74.0 2.9 %copy-start.6 = (f32[640,384]{1,0:T(8,128)S(1)}, f32[640,384]{1,0:T(8,128)}, u32[]{:S(2)}) copy-start(f32[640,384]{1,0:T(8,128)} %get-tuple-element.40) | copy-start | bytes 2949124
where the time goes:
time: 82 us; the launch traced here: 81.1 us
  Pallas kernels  60.1 us (73%)
  local copies, waits for them, and re-layouts  20.3 us (25%)
    pallas_call x1, Pallas kernels, local(): pl.pallas_call(kernel, out_shape=(shape(buses), jax.ShapeDtypeStruct((1,...  60.1 us
    unnamed x32, local copies, waits for them, and re-layouts  18.9 us

commit v1 on v0

v1 whole, which is shorter than its diff:
```python
import jax
import jax.numpy as jnp
from jax import lax
from jax.experimental import pallas as pl
from jax.experimental.pallas import tpu as pltpu
from jax.sharding import PartitionSpec as P

MESH = pl.DeviceIdType.MESH
PRIMAL = 0.4
DUAL = 0.4
W = 128
F32 = jnp.float32
BF16 = jnp.bfloat16


def split(values):
    hi = values.astype(BF16)
    lo = (values - hi.astype(F32)).astype(BF16)
    return jnp.concatenate([hi, lo], axis=1)


def joined(product):
    return product[:, :W] + product[:, W:]


def dot(a, b):
    return jnp.dot(a, b, preferred_element_type=F32)


def columns(row):
    blocks = []
    for i in range(row.shape[1] // W):
        blocks.append(jnp.transpose(jnp.broadcast_to(row[:, i * W : (i + 1) * W], (W, W))))
    return jnp.concatenate(blocks, axis=0) if len(blocks) > 1 else blocks[0]


def wide(block, count):
    return jnp.concatenate([block] * count, axis=1) if count > 1 else block


def make_kernel(sizes):
    buses, plants, lines, cuts, cells, hours, times, zones = sizes
    chunks = hours // W
    pad = -(-plants // W) * W
    prow = -(-plants // 16) * 16
    srow = -(-plants // 8) * 8
    parts = 4
    depth = cells // parts
    L0, F0, P0 = 0, lines, lines + cuts
    T0 = P0 + pad
    rows = T0 + cuts
    mid = times // 4
    c_gen, c_line, c_cut, c_sto = 0, buses, buses + lines, buses + lines + cuts
    c_rows = c_sto + pad
    cap_step = PRIMAL / (hours * times)

    def kernel(
        h_cell, h_pl, h_sto, h_to, h_from, h_lcap, h_cfrom, h_cto, h_ccap, h_gcost, h_ccost, h_cap,
        h_dem, h_av, h_run, h_gen, h_rel, h_lev, h_lf, h_cf, h_bal, h_dc, h_ds,
        o_gen, o_cap, o_rel, o_lev, o_lf, o_cf, o_bal, o_dc, o_ds,
        cell, r_pl, r_sto, r_to, r_from, r_lcap, r_cfrom, r_cto, r_ccap, r_gcost, r_ccost, r_cap,
        dem, av, run, gen, rel, lev, lf, cf, bal, dc, ds,
        inc, inct, bars, gbar, lbar, colf, padr, p_pl, p_sto, dcut, far, near, own,
        x_ct, x_ds, x_lb, s_p, x_p, s_b, x_b, x_far, x_inf, slot_a, slot_b,
        isem, ct_s, ct_r, ds_s, ds_r, lb_s, lb_r, p_s, p_r, b_s, b_r, far_s, far_r, inf_s, inf_r, pa_s, pa_r, pb_s, pb_r,
    ):
        t = lax.axis_index("tm")
        q = lax.axis_index("net")
        qn = lax.rem(q + 1, zones)
        qp = lax.rem(q + zones - 1, zones)
        sign = 1 - 2 * lax.rem(q, 2)
        mate = q + sign
        far_zone = lax.rem(q - sign + zones, zones)
        far_to = lax.rem(q - 2 * sign + zones, zones)
        tn = lax.rem(t + 1, times)
        tp = lax.rem(t + times - 1, times)

        loads = {}
        pairs = [
            ("cell", h_cell, cell), ("cto", h_cto, r_cto), ("to", h_to, r_to),
            ("from", h_from, r_from), ("cfrom", h_cfrom, r_cfrom), ("pl", h_pl, r_pl),
            ("gcost", h_gcost, r_gcost), ("lcap", h_lcap, r_lcap), ("ccap", h_ccap, r_ccap),
            ("sto", h_sto, r_sto), ("ccost", h_ccost, r_ccost), ("cap", h_cap, r_cap),
            ("av", h_av, av), ("dc", h_dc, dc),
        ]
        for k in range(parts):
            at = pl.ds(k * depth, depth)
            pairs.append((("run", k), h_run.at[at], run.at[at]))
        pairs += [
            ("ds", h_ds, ds), ("bal", h_bal, bal), ("lf", h_lf, lf), ("cf", h_cf, cf),
            ("gen", h_gen, gen), ("rel", h_rel, rel), ("lev", h_lev, lev), ("dem", h_dem, dem),
        ]
        for n, (name, src, dst) in enumerate(pairs):
            loads[name] = pltpu.make_async_copy(src, dst, isem.at[n])
            loads[name].start()

        barrier = pltpu.get_barrier_semaphore()

        core = lax.rem(t, 2)
        z = lax.rem(t // 2, mid)
        y = t // (2 * mid)

        def square(i):
            return ((1 - y if i // 2 else y) * mid + z) * 2 + (1 - core if i % 2 else core)

        def along(i):
            return (y * mid + lax.rem(z + i, mid)) * 2 + core

        def greet(tt, qq):
            pl.semaphore_signal(barrier, inc=1, device_id=(tt, qq), device_id_type=MESH)

        for d in (1, 2, zones - 2, zones - 1):
            greet(t, lax.rem(q + d, zones))
        for i in range(1, 4):
            greet(square(i), q)
        greet(lax.rem(t + 2 * core - 1 + times, times), q)
        for i in range(1, mid):
            greet(along(i), q)

        sent = []

        def send(src, dst, ssem, rsem, tt, qq):
            copy = pltpu.make_async_remote_copy(
                src_ref=src, dst_ref=dst, send_sem=ssem, recv_sem=rsem,
                device_id=(tt, qq), device_id_type=MESH,
            )
            copy.start()
            sent.append(copy)
            return copy

        def lanes(c):
            return slice(c * W, (c + 1) * W)

        def price_row(dual_of):
            total = None
            for c in range(chunks):
                term = av[:, lanes(c)] * dual_of(c)
                total = term if total is None else total + term
            return jnp.concatenate(
                [
                    jnp.sum(jnp.transpose(total[i * W : (i + 1) * W]), axis=0, keepdims=True)
                    for i in range(buses // W)
                ],
                axis=1,
            )

        def price_copy(slot, k, i, ssem, rsem, tt):
            return pltpu.make_async_remote_copy(
                src_ref=slot.at[k, 0], dst_ref=slot.at[k, i], send_sem=ssem.at[k],
                recv_sem=rsem.at[k], device_id=(tt, q), device_id_type=MESH,
            )

        def price_wait(slot, k, count, ssem, rsem, tt):
            everyone = slot.at[k, pl.ds(1, count - 1)]
            whole = pltpu.make_async_remote_copy(
                src_ref=everyone, dst_ref=everyone, send_sem=ssem.at[k], recv_sem=rsem.at[k],
                device_id=(tt, q), device_id_type=MESH,
            )
            whole.wait_recv()
            whole.wait_send()

        def price_first(k, row):
            slot_a[k, 0] = row
            for i in range(1, 4):
                price_copy(slot_a, k, i, pa_s, pa_r, square(i)).start()

        def price_second(k):
            price_wait(slot_a, k, 4, pa_s, pa_r, square(1))
            total = None
            for yy in (0, 1):
                for cc in (0, 1):
                    term = slot_a[k, (1 - y if yy else y) * 2 + (1 - core if cc else core)]
                    total = term if total is None else total + term
            slot_b[k, 0] = total
            for i in range(1, mid):
                price_copy(slot_b, k, i, pb_s, pb_r, along(i)).start()

        def price_all(k):
            price_wait(slot_b, k, mid, pb_s, pb_r, along(1))
            total = slot_b[k, lax.rem(z + mid, mid)]
            for j in range(1, mid):
                total = total + slot_b[k, lax.rem(z - j + mid, mid)]
            return total

        lane_bus = lax.broadcasted_iota(jnp.int32, (W, buses), 1)
        row_bus = lax.broadcasted_iota(jnp.int32, (buses, W), 0)
        one, zero = F32(1.0), F32(0.0)

        def flags(mask):
            return jnp.where(mask, one, zero)

        def place(at, to_row, from_row):
            m = jnp.zeros((W, buses), F32)
            mt = jnp.zeros((buses, W), F32)
            if to_row is not None:
                m = m + flags(wide(columns(to_row), buses // W) == lane_bus)
                mt = mt + flags(to_row == row_bus)
            if from_row is not None:
                m = m - flags(wide(columns(from_row), buses // W) == lane_bus)
                mt = mt - flags(from_row == row_bus)
            inc[at : at + W, :] = m.astype(BF16)
            inct[:, at : at + W] = mt.astype(BF16)

        for name in ("cto", "to", "from", "cfrom", "pl", "gcost", "lcap", "ccap", "sto", "ccost", "cap", "cell"):
            loads[name].wait()
        p_pl[...] = jnp.full_like(p_pl, -1)
        p_pl[:, 0:plants] = r_pl[...]
        p_sto[...] = jnp.zeros_like(p_sto)
        p_sto[:, 0:plants] = r_sto[...]
        for i in range(lines // W):
            place(L0 + i * W, r_to[i : i + 1, :], r_from[i : i + 1, :])
            colf[c_line + i * W : c_line + (i + 1) * W, :] = columns(r_lcap[i : i + 1, :])
        for i in range(cuts // W):
            place(F0 + i * W, None, r_cfrom[:, i * W : (i + 1) * W])
        for i in range(pad // W):
            place(P0 + i * W, p_pl[:, i * W : (i + 1) * W], None)
        for at, row in ((c_gen, r_gcost), (c_cut, r_ccap), (c_sto, p_sto)):
            colf[at : at + row.shape[1], :] = columns(row[...])
        padr[...] = jnp.zeros_like(padr)

        k_p, k_b = [], []

        def send_prices(k, c, value):
            s_p[k, c] = joined(dot(inc[T0:rows, :], value))
            k_p.append(send(s_p.at[k, c], x_p.at[k, c], p_s.at[k, c], p_r.at[k, c], t, qp))

        def terms(zone, out):
            ids = lax.broadcasted_iota(jnp.int32, (prow, depth), 0) + zone * plants
            total = None
            for k in range(parts):
                if ("run", k) in loads:
                    loads.pop(("run", k)).wait()
                onehot = flags(ids == cell[:, k * depth : (k + 1) * depth]).astype(BF16)
                term = dot(onehot, run[k * depth : (k + 1) * depth, :])
                total = term if total is None else total + term
            for c in range(chunks):
                out[c] = total[:, lanes(c)]

        loads["av"].wait()
        loads["dc"].wait()
        row = price_row(lambda c: dc[:, lanes(c)])
        terms(far_zone, far)
        loads["ds"].wait()

        pl.semaphore_wait(barrier, mid + 7)
        k_ct = send(r_cto, x_ct, ct_s, ct_r, t, qn)
        k_far = [
            send(far.at[c, pl.ds(0, srow)], x_far.at[c], far_s.at[c], far_r.at[c], t, far_to)
            for c in range(chunks)
        ]
        k_ds = [send(ds.at[:, pl.ds(0, W)], x_ds.at[0], ds_s.at[0], ds_r.at[0], tp, q)]
        price_first(0, row)
        terms(mate, near)

        k_ct.wait_recv()
        for i in range(cuts // W):
            place(T0 + i * W, x_ct[:, i * W : (i + 1) * W], None)
        loads["bal"].wait()
        for c in range(chunks):
            send_prices(0, c, split(bal[:, lanes(c)]))

        def bound(v, b):
            return jnp.minimum(jnp.maximum(v, -b), b)

        def line_step(c, value, flow, flow_out):
            diff = joined(dot(inc[L0:P0, :], value))
            cap = colf[c_line : c_line + lines, :]
            old = flow[:, lanes(c)]
            new = bound(old + PRIMAL * diff[:lines], cap)
            bars[c, L0 : L0 + lines, :] = split(2.0 * new - old)
            flow_out[:, lanes(c)] = new
            dcut[:, lanes(c)] = diff[lines:]

        def cut_step(k, c, flow, flow_out):
            k_p[k * chunks + c].wait_recv()
            cap = colf[c_cut : c_cut + cuts, :]
            old = flow[:, lanes(c)]
            new = bound(old + PRIMAL * (x_p[k, c] + dcut[:, lanes(c)]), cap)
            bar = 2.0 * new - old
            flow_out[:, lanes(c)] = new
            s_b[k, c] = bar
            k_b.append(send(s_b.at[k, c], x_b.at[k, c], b_s.at[k, c], b_r.at[k, c], t, qn))
            bars[c, F0 : F0 + cuts, :] = split(bar)

        def cut_in(k, c, out_ref):
            k_b[k * chunks + c].wait_recv()
            more = joined(dot(inct[:, T0:rows], split(x_b[k, c])))
            out_ref[:, lanes(c)] = out_ref[:, lanes(c)] - DUAL * more

        def plant_prices(c, value):
            return joined(dot(inc[P0 : P0 + pad, :], value))[:plants]

        def release_step(c, price, old_ref, dual_ref, out_ref):
            old = old_ref[:, lanes(c)]
            new = jnp.maximum(0.0, old + PRIMAL * (price + dual_ref[:, lanes(c)]))
            bar = 2.0 * new - old
            out_ref[:, lanes(c)] = new
            padr[0:plants, :] = bar
            bars[c, P0 : P0 + pad, :] = split(padr[...])
            return bar

        def gen_step(c, old_ref, price_ref, dual_ref, out_ref):
            cost = colf[c_gen : c_gen + buses, :]
            old = old_ref[:, lanes(c)]
            new = jnp.maximum(
                0.0, old - PRIMAL * (cost - price_ref[:, lanes(c)] + dual_ref[:, lanes(c)])
            )
            gbar[:, lanes(c)] = 2.0 * new - old
            out_ref[:, lanes(c)] = new

        lane = lax.broadcasted_iota(jnp.int32, (plants, W), 1)

        def level_step(k, dual_ref, old_ref, out_ref):
            cap = colf[c_sto : c_sto + pad, :][:plants]
            rolled = [pltpu.roll(dual_ref[:, lanes(c)], W - 1, 1) for c in range(chunks)]
            rolled.append(pltpu.roll(x_ds[k], W - 1, 1))
            for c in range(chunks):
                after = jnp.where(lane == W - 1, rolled[c + 1], rolled[c])
                old = old_ref[:, lanes(c)]
                new = jnp.minimum(
                    jnp.maximum(old + PRIMAL * (dual_ref[:, lanes(c)] - after), 0.0), cap
                )
                lbar[k, :, lanes(c)] = 2.0 * new - old
                out_ref[:, lanes(c)] = new
            return send(
                lbar.at[k, :, pl.ds(hours - W, W)], x_lb.at[k], lb_s.at[k], lb_r.at[k], tn, q
            )

        def storage_step(k, dual_ref, relbars, out_ref):
            rolled = [pltpu.roll(x_lb[k], 1, 1)]
            rolled += [pltpu.roll(lbar[k, :, lanes(c)], 1, 1) for c in range(chunks)]
            for c in range(chunks):
                before = jnp.where(lane == 0, rolled[c], rolled[c + 1])
                inflow = own[c][:plants]
                out_ref[:, lanes(c)] = dual_ref[:, lanes(c)] + DUAL * (
                    inflow - lbar[k, :, lanes(c)] + before - relbars(c)
                )

        def balance_step(c, old_ref, out_ref):
            balance = gbar[:, lanes(c)] + joined(dot(inct[:, 0:T0], bars[c]))
            out_ref[:, lanes(c)] = old_ref[:, lanes(c)] + DUAL * (dem[:, lanes(c)] - balance)

        def cap_dual_step(cap_bar, dual_ref, out_ref):
            col = columns(cap_bar)
            for c in range(chunks):
                out_ref[:, lanes(c)] = jnp.maximum(
                    0.0,
                    dual_ref[:, lanes(c)] - DUAL * (av[:, lanes(c)] * col - gbar[:, lanes(c)]),
                )

        def send_inflow(c):
            k_far[c].wait_recv()
            near[c, 0:srow, :] = near[c, 0:srow, :] + x_far[c]
            k_inf.append(
                send(near.at[c, pl.ds(0, srow)], x_inf.at[c], inf_s.at[c], inf_r.at[c], t, mate)
            )

        k_inf = []
        loads["lf"].wait()
        for c in range(chunks):
            line_step(c, split(bal[:, lanes(c)]), lf, o_lf)
        loads["cf"].wait()
        cut_step(0, 0, cf, o_cf)
        loads["gen"].wait()
        for c in range(chunks):
            gen_step(c, gen, bal, dc, o_gen)
        send_inflow(0)
        cut_step(0, 1, cf, o_cf)
        price_second(0)
        loads["rel"].wait()
        for c in range(chunks):
            release_step(c, plant_prices(c, split(bal[:, lanes(c)])), rel, ds, o_rel)
        send_inflow(1)
        cut_step(0, 2, cf, o_cf)
        loads["dem"].wait()
        for c in range(chunks):
            balance_step(c, bal, o_bal)
            cut_in(0, c, o_bal)
            send_prices(1, c, split(o_bal[:, lanes(c)]))
        send_inflow(2)

        loads["lev"].wait()
        k_ds[0].wait_recv()
        k_lb = [level_step(0, ds, lev, o_lev)]
        cost = r_ccost[...]
        cap_old = r_cap[...]
        cap_one = jnp.maximum(0.0, cap_old - cap_step * (cost - price_all(0)))
        cap_dual_step(2.0 * cap_one - cap_old, dc, o_dc)
        price_first(1, price_row(lambda c: o_dc[:, lanes(c)]))

        for c in range(chunks):
            line_step(c, split(o_bal[:, lanes(c)]), o_lf, o_lf)
            cut_step(1, c, o_cf, o_cf)
        price_second(1)
        for c in range(chunks):
            gen_step(c, o_gen, o_bal, o_dc, o_gen)
        terms(q, own)
        for c in range(chunks):
            k_inf[c].wait_recv()
            own[c, 0:srow, :] = own[c, 0:srow, :] + x_inf[c]
        k_lb[0].wait_recv()
        storage_step(0, ds, lambda c: 2.0 * o_rel[:, lanes(c)] - rel[:, lanes(c)], o_ds)
        k_ds.append(send(o_ds.at[:, pl.ds(0, W)], x_ds.at[1], ds_s.at[1], ds_r.at[1], tp, q))
        relbar = [
            release_step(c, plant_prices(c, split(o_bal[:, lanes(c)])), o_rel, o_ds, o_rel)
            for c in range(chunks)
        ]
        k_ds[1].wait_recv()
        k_lb.append(level_step(1, o_ds, o_lev, o_lev))
        for c in range(chunks):
            balance_step(c, o_bal, o_bal)
        cap_two = jnp.maximum(0.0, cap_one - cap_step * (cost - price_all(1)))
        o_cap[...] = cap_two
        cap_dual_step(2.0 * cap_two - cap_one, o_dc, o_dc)
        for c in range(chunks):
            cut_in(1, c, o_bal)
        k_lb[1].wait_recv()
        k_ds[1].wait_send()
        storage_step(1, o_ds, lambda c: relbar[c], o_ds)
        for copy in sent:
            if copy is not k_ds[1]:
                copy.wait_send()

    def big(n, kind=F32):
        return pltpu.VMEM((n, hours), kind)

    dma = pltpu.SemaphoreType.DMA
    def row(n, kind=F32):
        return pltpu.VMEM((1, n), kind)

    def lrow(kind):
        return pltpu.VMEM((lines // W, W), kind)

    i32 = jnp.int32
    scratch = [
        row(cells, i32), row(plants, i32), row(plants), lrow(i32), lrow(i32), lrow(F32),
        row(cuts, i32), row(cuts, i32), row(cuts), row(buses), row(buses), row(buses),
        big(buses), big(buses), big(cells, BF16), big(buses), big(plants), big(plants),
        big(lines), big(cuts), big(buses), big(buses), big(plants),
        pltpu.VMEM((rows, buses), BF16),
        pltpu.VMEM((buses, rows), BF16),
        pltpu.VMEM((chunks, rows - cuts, 2 * W), BF16),
        big(buses),
        pltpu.VMEM((2, plants, hours), F32),
        pltpu.VMEM((c_rows, W), F32),
        pltpu.VMEM((pad, W), F32),
        row(pad, i32), row(pad),
        big(cuts),
        pltpu.VMEM((chunks, prow, W), F32),
        pltpu.VMEM((chunks, prow, W), F32),
        pltpu.VMEM((chunks, prow, W), F32),
        pltpu.VMEM((1, cuts), jnp.int32),
        pltpu.VMEM((2, plants, W), F32),
        pltpu.VMEM((2, plants, W), F32),
        pltpu.VMEM((2, chunks, cuts, W), F32),
        pltpu.VMEM((2, chunks, cuts, W), F32),
        pltpu.VMEM((2, chunks, cuts, W), F32),
        pltpu.VMEM((2, chunks, cuts, W), F32),
        pltpu.VMEM((chunks, srow, W), F32),
        pltpu.VMEM((chunks, srow, W), F32),
        pltpu.VMEM((2, 4, 1, buses), F32),
        pltpu.VMEM((2, mid, 1, buses), F32),
        dma((22 + parts,)),
        dma, dma, dma((2,)), dma((2,)), dma((2,)), dma((2,)),
        dma((2, chunks)), dma((2, chunks)), dma((2, chunks)), dma((2, chunks)),
        dma((chunks,)), dma((chunks,)), dma((chunks,)), dma((chunks,)),
        dma((2,)), dma((2,)), dma((2,)), dma((2,)),
    ]
    return kernel, scratch


def write_out(*refs):
    count = len(refs) // 2
    sem = refs[-1]
    copies = [
        pltpu.make_async_copy(refs[i], refs[count + i], sem.at[i]) for i in range(count)
    ]
    for copy in copies:
        copy.start()
    for copy in copies:
        copy.wait()


def solution(mesh):
    times, zones = mesh.shape["tm"], mesh.shape["net"]

    def local(
        demand, availability, gen_cost, cap_cost, runoff, cell_plant, plant_bus, store_cap,
        line_from, line_to, line_cap, cut_from, cut_to, cut_cap, generation, capacity,
        release, storage_level, line_flow, cut_flow, dual_bal, dual_cap, dual_sto,
    ):
        buses, hours = demand.shape
        plants, lines, cuts, cells = (
            release.shape[0], line_flow.shape[0], cut_flow.shape[0], runoff.shape[0],
        )
        kernel, scratch = make_kernel((buses, plants, lines, cuts, cells, hours, times, zones))
        hbm = pl.BlockSpec(memory_space=pltpu.HBM)
        shapes = [(n, hours) for n in (buses, 0, plants, plants, lines, cuts, buses, buses, plants)]
        shapes[1] = (1, buses)

        def row(values):
            return values.reshape(1, -1)

        def tiles(values):
            return values.reshape(-1, W)

        outs = pl.pallas_call(
            kernel,
            out_shape=tuple(pltpu.VMEM(shape, F32) for shape in shapes),
            in_specs=[hbm] * 23,
            out_specs=(pl.BlockSpec(memory_space=pltpu.VMEM),) * 9,
            scratch_shapes=scratch,
            compiler_params=pltpu.CompilerParams(
                collective_id=0, has_side_effects=True, vmem_limit_bytes=59 << 20
            ),
        )(
            row(cell_plant), row(plant_bus), row(store_cap), tiles(line_to), tiles(line_from),
            tiles(line_cap), row(cut_from), row(cut_to), row(cut_cap), row(gen_cost), row(cap_cost),
            row(capacity),
            demand, availability, runoff, generation, release, storage_level, line_flow, cut_flow,
            dual_bal, dual_cap, dual_sto,
        )
        outs = pl.pallas_call(
            write_out,
            out_shape=tuple(jax.ShapeDtypeStruct(shape, F32) for shape in shapes),
            in_specs=[pl.BlockSpec(memory_space=pl.ANY)] * 9,
            out_specs=(hbm,) * 9,
            scratch_shapes=[pltpu.SemaphoreType.DMA((9,))],
            compiler_params=pltpu.CompilerParams(vmem_limit_bytes=1 << 20),
        )(*outs)
        outs = list(outs)
        outs[1] = outs[1].reshape(buses)
        return tuple(outs)

    both, net = P("net", "tm"), P("net")
    in_specs = (both, both, net, net, both) + (net,) * 9 + (both, net) + (both,) * 7
    out_specs = (both, net) + (both,) * 7
    return jax.shard_map(local, mesh=mesh, in_specs=in_specs, out_specs=out_specs, check_vma=False)
```

time: 82 us -> 59.1 us (0.72)
  local copies, waits for them, and re-layouts: 20.3 us -> 0 us
  Pallas kernels: 60.1 us -> 58.3 us
    unnamed x32 -> x0, local copies, waits for them, and re-layouts: 18.9 us -> none
    pallas_call x1 -> x2, Pallas kernels: 60.1 us -> 58.3 us  [the longest x1 56.1 us: local(): pl.pallas_call(kernel, out_shape=tuple((pltpu.VMEM(shape, F32) for shape...]
    concatenate x2 -> x0, local copies, waits for them, and re-layouts: 1.37 us -> none  [the longest x1 0.69 us: local(): jnp.concatenate([line_to, line_from, cut_from, cut_to, jnp.pad(plant_bus,...]
where the time goes in v1:
time: 59.1 us; the launch traced here: 59 us
  Pallas kernels  58.3 us (99%)
  between operations  0.66 us (1%)
    pallas_call x1, Pallas kernels, local(): pl.pallas_call(kernel, out_shape=tuple((pltpu.VMEM(shape, F32) for shape...  56.1 us
    pallas_call x1, Pallas kernels, local(): pl.pallas_call(write_out, out_shape=tuple((jax.ShapeDtypeStruct(shape, F3...  2.22 us

profile of v1, /device:TPU:2, one launch (start us, length us, event | category | flops | bytes accessed | tf_op | source)
XLA Modules:
  0.0 59.0 jit_solution(5110133271649629895)
XLA Ops:
  0.7 56.1 %shard_map.286 = (f32[512,384]{1,0:T(8,128)S(1)}, f32[1,512]{1,0:T(1,128)S(1)}, f32[225,384]{1,0:T(8,128)S(1)}, f32[225,384]{1,0:T(8,128)S(1)}, f32[640,384]{1,0...) custom-call(s32[1,4096]{1,0:T(1,128)} %bitcast.13, ...), custom_call_target="tpu_custom_call" | custom-call | tf_op jit(solution)/shard_map/pallas_call | solution.py:507
  56.7 2.2 %shard_map.287 = (f32[512,384]{1,0:T(8,128)}, f32[1,512]{1,0:T(1,128)}, f32[225,384]{1,0:T(8,128)}, f32[225,384]{1,0:T(8,128)}, f32[640,384]{1,0:T(8,128)}, /*in...) custom-call(f32[512,384]{1,0:T(8,128)S(1)} %get-tuple-element.27.refs_0_, ...), custom_call_target="tpu_custom_call" | custom-call | tf_op jit(solution)/shard_map/pallas_call | solution.py:523

commit v2 on v1

--- a/solution.py
+++ b/solution.py
@@ -81,13 +81,13 @@
             ("from", h_from, r_from), ("cfrom", h_cfrom, r_cfrom), ("pl", h_pl, r_pl),
             ("gcost", h_gcost, r_gcost), ("lcap", h_lcap, r_lcap), ("ccap", h_ccap, r_ccap),
             ("sto", h_sto, r_sto), ("ccost", h_ccost, r_ccost), ("cap", h_cap, r_cap),
-            ("av", h_av, av), ("dc", h_dc, dc),
+            ("av", h_av, av), ("dc", h_dc, dc), ("ds", h_ds, ds), ("bal", h_bal, bal),
         ]
         for k in range(parts):
             at = pl.ds(k * depth, depth)
             pairs.append((("run", k), h_run.at[at], run.at[at]))
         pairs += [
-            ("ds", h_ds, ds), ("bal", h_bal, bal), ("lf", h_lf, lf), ("cf", h_cf, cf),
+            ("lf", h_lf, lf), ("cf", h_cf, cf),
             ("gen", h_gen, gen), ("rel", h_rel, rel), ("lev", h_lev, lev), ("dem", h_dem, dem),
         ]
         for n, (name, src, dst) in enumerate(pairs):
@@ -239,25 +239,28 @@
         loads["av"].wait()
         loads["dc"].wait()
         row = price_row(lambda c: dc[:, lanes(c)])
-        terms(far_zone, far)
         loads["ds"].wait()
 
         pl.semaphore_wait(barrier, mid + 7)
         k_ct = send(r_cto, x_ct, ct_s, ct_r, t, qn)
-        k_far = [
-            send(far.at[c, pl.ds(0, srow)], x_far.at[c], far_s.at[c], far_r.at[c], t, far_to)
-            for c in range(chunks)
-        ]
         k_ds = [send(ds.at[:, pl.ds(0, W)], x_ds.at[0], ds_s.at[0], ds_r.at[0], tp, q)]
         price_first(0, row)
-        terms(mate, near)
-
+        terms(far_zone, far)
+        k_far = []
+
+        def send_far(c):
+            k_far.append(
+                send(far.at[c, pl.ds(0, srow)], x_far.at[c], far_s.at[c], far_r.at[c], t, far_to)
+            )
+
+        loads["bal"].wait()
         k_ct.wait_recv()
         for i in range(cuts // W):
             place(T0 + i * W, x_ct[:, i * W : (i + 1) * W], None)
-        loads["bal"].wait()
         for c in range(chunks):
             send_prices(0, c, split(bal[:, lanes(c)]))
+        for c in range(chunks):
+            send_far(c)
 
         def bound(v, b):
             return jnp.minimum(jnp.maximum(v, -b), b)
@@ -359,42 +362,44 @@
         loads["lf"].wait()
         for c in range(chunks):
             line_step(c, split(bal[:, lanes(c)]), lf, o_lf)
+        loads["gen"].wait()
+        for c in range(chunks):
+            gen_step(c, gen, bal, dc, o_gen)
         loads["cf"].wait()
         cut_step(0, 0, cf, o_cf)
-        loads["gen"].wait()
-        for c in range(chunks):
-            gen_step(c, gen, bal, dc, o_gen)
-        send_inflow(0)
-        cut_step(0, 1, cf, o_cf)
-        price_second(0)
         loads["rel"].wait()
         for c in range(chunks):
             release_step(c, plant_prices(c, split(bal[:, lanes(c)])), rel, ds, o_rel)
-        send_inflow(1)
-        cut_step(0, 2, cf, o_cf)
         loads["dem"].wait()
         for c in range(chunks):
+            if c:
+                cut_step(0, c, cf, o_cf)
             balance_step(c, bal, o_bal)
+        for c in range(chunks):
             cut_in(0, c, o_bal)
             send_prices(1, c, split(o_bal[:, lanes(c)]))
-        send_inflow(2)
-
+        terms(mate, near)
+        for c in range(chunks):
+            send_inflow(c)
+        price_second(0)
+
+        for c in range(chunks):
+            line_step(c, split(o_bal[:, lanes(c)]), o_lf, o_lf)
+        cut_step(1, 0, o_cf, o_cf)
         loads["lev"].wait()
         k_ds[0].wait_recv()
         k_lb = [level_step(0, ds, lev, o_lev)]
+        cut_step(1, 1, o_cf, o_cf)
         cost = r_ccost[...]
         cap_old = r_cap[...]
         cap_one = jnp.maximum(0.0, cap_old - cap_step * (cost - price_all(0)))
         cap_dual_step(2.0 * cap_one - cap_old, dc, o_dc)
+        cut_step(1, 2, o_cf, o_cf)
         price_first(1, price_row(lambda c: o_dc[:, lanes(c)]))
-
-        for c in range(chunks):
-            line_step(c, split(o_bal[:, lanes(c)]), o_lf, o_lf)
-            cut_step(1, c, o_cf, o_cf)
-        price_second(1)
         for c in range(chunks):
             gen_step(c, o_gen, o_bal, o_dc, o_gen)
         terms(q, own)
+        price_second(1)
         for c in range(chunks):
             k_inf[c].wait_recv()
             own[c, 0:srow, :] = own[c, 0:srow, :] + x_inf[c]

time: 59.1 us -> 56.8 us (0.961); the launches traced: 59 us -> 55.9 us
  Pallas kernels: 58.3 us -> 55.2 us
    pallas_call x1, Pallas kernels: 56.1 us -> 53 us  [local(): pl.pallas_call(kernel, out_shape=tuple((pltpu.VMEM(shape, F32) for shape...]
where the time goes in v2:
time: 56.8 us; the launch traced here: 55.9 us
  Pallas kernels  55.2 us (97%)
  between operations  0.66 us (1%)
    pallas_call x1, Pallas kernels, local(): pl.pallas_call(kernel, out_shape=tuple((pltpu.VMEM(shape, F32) for shape...  53 us
    pallas_call x1, Pallas kernels, local(): pl.pallas_call(write_out, out_shape=tuple((jax.ShapeDtypeStruct(shape, F3...  2.22 us

profile of v2, /device:TPU:2, one launch (start us, length us, event | category | flops | bytes accessed | tf_op | source)
XLA Modules:
  0.0 55.9 jit_solution(13344925425589498720)
XLA Ops:
  0.7 53.0 %shard_map.286 = (f32[512,384]{1,0:T(8,128)S(1)}, f32[1,512]{1,0:T(1,128)S(1)}, f32[225,384]{1,0:T(8,128)S(1)}, f32[225,384]{1,0:T(8,128)S(1)}, f32[640,384]{1,0...) custom-call(s32[1,4096]{1,0:T(1,128)} %bitcast.13, ...), custom_call_target="tpu_custom_call" | custom-call | tf_op jit(solution)/shard_map/pallas_call | solution.py:512
  53.7 2.2 %shard_map.287 = (f32[512,384]{1,0:T(8,128)}, f32[1,512]{1,0:T(1,128)}, f32[225,384]{1,0:T(8,128)}, f32[225,384]{1,0:T(8,128)}, f32[640,384]{1,0:T(8,128)}, /*in...) custom-call(f32[512,384]{1,0:T(8,128)S(1)} %get-tuple-element.27.refs_0_, ...), custom_call_target="tpu_custom_call" | custom-call | tf_op jit(solution)/shard_map/pallas_call | solution.py:528
